TPU v7x, 512 devices: a whole 4x8x8 slice. The times are simulated.
512 devices in a mesh: walk: 32 (over z, y_hi, core), pb: 16 (over y_lo, x).
Axes of the slice: x: 4, y: 8 (y_hi: 2, y_lo: 4; y = y_hi * 4 + y_lo), z: 8, core: 2. Of those that a mesh axis runs over, the one named last changes fastest.
Arguments:
- bras: bfloat16 [256, 4, 4, 208], P('walk'), may hold values from -6 to 6
- fields: float32 [1, 256, 4, 160], P(None, 'walk'), may hold values from -5 to 5
- chol: bfloat16 [16, 160, 21632], P('pb', 'walk'), may hold values from -0.0234375 to 0.0234375
- one_body: bfloat16 [4, 21632], replicated, may hold values from -0.4375 to 0.4375
- pair_table: int32 [16, 2], replicated, may hold values from 0 to 3, as said below
- kpq_map: int32 [4, 4], replicated, may hold values from 0 to 3, as said below
Outputs:
- new_bras: bfloat16 [256, 4, 4, 208], P('walk')
Inputs may be any that keep to these rules, and one draw needn't show every extreme that they name: `pair_table`: each row holds a momentum transfer and a k-point; each of the 16 pairs stands in exactly one row. kpq_map[Q, k] is the sum k+Q of an abelian group on the 4 k-points; each row and each column is a permutation of the k-points.
All inputs are finite; a program needn't handle non-finite values.
Results may differ from a plain program's by a relative error of at most 0.009.
Values may be sent and summed in bfloat16 or wider, within the bound.
A program may use at most 64 MiB of HBM per device.

v0:
```python
import jax
import jax.numpy as jnp
from jax import lax
from jax.sharding import PartitionSpec as P

ORDER = 4


def select_pairs(pair_table, kpq_map, first_pair, pair_count, kpoints):
    owned = lax.dynamic_slice_in_dim(pair_table, first_pair, pair_count, 0)
    charges = owned[:, 0]
    kblocks = owned[:, 1]
    levels = jnp.arange(kpoints, dtype=jnp.int32)
    charge_hot = (charges[:, None] == levels[None, :]).astype(jnp.int32)
    block_hot = (kblocks[:, None] == levels[None, :]).astype(jnp.int32)
    targets = jnp.sum(
        charge_hot[:, :, None] * block_hot[:, None, :] * kpq_map[None, :, :], axis=(1, 2)
    )
    target_hot = (targets[:, None] == levels[None, :]).astype(jnp.float32)
    return (charges, kblocks, target_hot)


def split_terms(current_term, kblocks, orbitals):
    walkers, _, occupied, _ = current_term.shape
    chosen = jnp.take(current_term, kblocks, axis=1)
    chosen = chosen.reshape(walkers, kblocks.shape[0], occupied, 2, orbitals)
    return jnp.transpose(chosen, (1, 3, 0, 2, 4)).astype(jnp.float32)


def contract_slab(halves, field_rows, slab_piece):
    pair_count, slab_rows, flat_cols = slab_piece.shape
    orbitals = halves.shape[-1]
    weighted = (field_rows[:, None, :, None, :, None] * halves[:, :, :, :, None, :]).astype(
        jnp.bfloat16
    )
    weighted = weighted.reshape(pair_count, -1, slab_rows * orbitals)
    matrix = slab_piece.reshape(pair_count, slab_rows * orbitals, 2 * orbitals)
    return jnp.einsum("prk,pkd->prd", weighted, matrix, preferred_element_type=jnp.float32)


def join_product(product, walkers, occupied, orbitals):
    pair_count = product.shape[0]
    product = product.reshape(pair_count, 2, walkers, occupied, 2 * orbitals)
    real_part = product[:, 0, ..., :orbitals] - product[:, 1, ..., orbitals:]
    imag_part = product[:, 0, ..., orbitals:] + product[:, 1, ..., :orbitals]
    return jnp.concatenate([real_part, imag_part], axis=-1)


def combine_blocks(contrib, every_hot):
    by_target = jnp.einsum("pk,pwix->wkix", every_hot, contrib, precision=lax.Precision.HIGHEST)
    return lax.psum(by_target, "pb")


def one_body_step(sectioned, one_body, orbitals):
    matrix = one_body.reshape(one_body.shape[0], orbitals, 2 * orbitals)
    real_half = sectioned[..., :orbitals]
    imag_half = sectioned[..., orbitals:]
    first_half = jnp.einsum("wkin,knd->wkid", real_half, matrix, preferred_element_type=jnp.float32)
    second_half = jnp.einsum(
        "wkin,knd->wkid", imag_half, matrix, preferred_element_type=jnp.float32
    )
    real_part = first_half[..., :orbitals] - second_half[..., orbitals:]
    imag_part = first_half[..., orbitals:] + second_half[..., :orbitals]
    return jnp.concatenate([real_part, imag_part], axis=-1).astype(jnp.bfloat16)


def shards(bras, fields, chol, one_body, pair_table, kpq_map):
    walkers, kpoints, occupied, doubled = bras.shape
    orbitals = doubled // 2
    pair_count = chol.shape[0]
    first_pair = lax.axis_index("pb") * pair_count
    charges, kblocks, target_hot = select_pairs(
        pair_table, kpq_map, first_pair, pair_count, kpoints
    )
    stored = None
    bra_state = bras
    for saved_step in reversed(range(fields.shape[0])):
        field_rows = jnp.transpose(jnp.take(fields[saved_step], charges, axis=1), (1, 0, 2))
        current_term = bra_state
        summed_terms = bra_state.astype(jnp.float32)
        for taylor in range(1, ORDER + 1):
            halves = split_terms(current_term, kblocks, orbitals)
            if stored is None:
                stored = lax.all_gather(chol, "walk", axis=1, tiled=True)
                product = contract_slab(halves, field_rows, stored)
            else:
                product = contract_slab(halves, field_rows, stored)
            contrib = join_product(product, walkers, occupied, orbitals)
            scaled = combine_blocks(contrib, target_hot) / float(taylor)
            summed_terms = summed_terms + scaled
            current_term = scaled.astype(jnp.bfloat16)
        sectioned = summed_terms.astype(jnp.bfloat16)
        bra_state = one_body_step(sectioned, one_body, orbitals)
    return bra_state


def solution(mesh):
    return jax.shard_map(
        shards,
        mesh=mesh,
        in_specs=(
            P("walk", None, None, None),
            P(None, "walk", None, None),
            P("pb", "walk", None),
            P(),
            P(),
            P(),
        ),
        out_specs=P("walk", None, None, None),
        check_vma=False,
    )
```

profile of v0, /device:TPU:1, one launch (start us, length us, event | category | flops | bytes accessed | tf_op | source)
XLA Modules:
  0.0 938.7 jit_solution(4173836583247186828)
XLA Ops:
  6.5 2.1 copy.27
  8.7 0.0 all-gather.2.cloned.1.call-update
  8.7 0.0 all-reduce.5.cloned.1.call-start
  8.8 0.8 constant_dynamic-slice_fusion.1
  9.5 0.6 fusion.42
  14.1 0.7 select_convert_fusion
  14.9 0.1 reshape.593
  15.0 0.0 copy-done
  15.0 0.6 multiply_convert_fusion.3
  15.7 4.5 convert_element_type.131
  20.2 1.3 compare_convert_fusion.1
  21.6 0.7 multiply_reduce_fusion
  22.3 0.6 fusion.41
  22.9 164.4 %all-gather.2.cloned.1.call-done = bf16[1,160,21632]{2,0,1:T(2,128)(2,1)} async-done(((bf16[1,5,21632]{2,0,1:T(2,128)(2,1)}), bf16[1,160,21632]{2,0,1:T(2,128)(2,1)}) %all-gather.2.cloned.1.call-update) | async-done | bytes 6922256 | tf_op jit(solution)/shard_map/all_gather | solution.py:84
  187.3 43.1 %reduce.2 = bf16[160,21632]{1,0:T(8,128)(2,1)} reduce(bf16[1,160,21632]{2,0,1:T(2,128)(2,1)} %all-gather.2.cloned.1.call-done, bf16[]{:T(256)} %constant.109), dimensions={0}, to_apply=%all_gather.3.reduce_sub_computation | reduce | bytes 13844482 | tf_op jit(solution)/shard_map/all_gather | solution.py:84
  230.4 16.0 %reshape.453 = bf16[16640,208]{1,0:T(8,128)(2,1)} reshape(bf16[160,21632]{1,0:T(8,128)(2,1)} %reduce.2) | data formatting | bytes 13844480 | tf_op jit(solution)/shard_map/reshape.7
  246.4 0.0 copy-done.1
  246.4 4.9 fusion.8
  251.4 0.1 fusion.39
  251.4 0.1 maximum_bitcast_fusion
  251.5 0.7 multiply_bitcast_fusion.3
  252.3 0.0 all-reduce.5.cloned.1.call-update
  252.3 0.0 all-reduce.7.cloned.1.call-start
  252.3 150.4 %all-reduce.5.cloned.1.call-done = f32[8,4,4,208]{3,0,2,1:T(8,128)} async-done(((f32[8,4,4,208]{3,0,2,1:T(8,128)}), f32[8,4,4,208]{3,0,2,1:T(8,128)}) %all-reduce.5.cloned.1.call-update) | async-done | bytes 106512 | tf_op jit(solution)/shard_map/psum | solution.py:51
  402.8 0.8 fusion.27
  403.5 0.1 reshape.594
  403.7 0.6 multiply_convert_fusion.2
  404.3 4.6 convert_element_type.138
  408.8 5.6 fusion.11
  414.4 0.1 fusion.37
  414.5 0.1 maximum_bitcast_fusion.1
  414.6 0.7 multiply_bitcast_fusion.2
  415.3 0.0 all-reduce.7.cloned.1.call-update
  415.4 0.2 all-reduce.9.cloned.1.call-start
  415.6 162.8 %all-reduce.7.cloned.1.call-done = f32[8,4,4,208]{3,0,2,1:T(8,128)} async-done(((f32[8,4,4,208]{3,0,2,1:T(8,128)}), f32[8,4,4,208]{3,0,2,1:T(8,128)}) %all-reduce.7.cloned.1.call-update) | async-done | bytes 106512 | tf_op jit(solution)/shard_map/psum | solution.py:51
  578.4 0.9 broadcast_multiply_fusion.1
  579.4 0.1 reshape.595
  579.5 0.6 multiply_convert_fusion.1
  580.1 4.6 convert_element_type.143
  584.6 5.6 fusion.14
  590.3 0.1 fusion.35
  590.3 0.1 maximum_bitcast_fusion.2
  590.4 0.7 multiply_bitcast_fusion.1
  591.2 0.0 all-reduce.9.cloned.1.call-update
  591.2 0.0 all-reduce.11.cloned.1.call-start
  591.2 162.8 %all-reduce.9.cloned.1.call-done = f32[8,4,4,208]{3,0,2,1:T(8,128)} async-done(((f32[8,4,4,208]{3,0,2,1:T(8,128)}), f32[8,4,4,208]{3,0,2,1:T(8,128)}) %all-reduce.9.cloned.1.call-update) | async-done | bytes 106512 | tf_op jit(solution)/shard_map/psum | solution.py:51
  754.0 0.9 broadcast_multiply_fusion
  755.0 0.1 reshape.596
  755.1 0.6 multiply_convert_fusion
  755.7 4.6 convert_element_type.148
  760.3 0.0 copy-start.6
  760.3 5.7 fusion.17
  765.9 0.1 fusion.33
  766.0 0.1 maximum_bitcast_fusion.3
  766.1 0.7 multiply_bitcast_fusion
  766.8 0.0 all-reduce.11.cloned.1.call-update
  766.9 0.4 reshape.610
  767.3 162.7 %all-reduce.11.cloned.1.call-done = f32[8,4,4,208]{3,0,2,1:T(8,128)} async-done(((f32[8,4,4,208]{3,0,2,1:T(8,128)}), f32[8,4,4,208]{3,0,2,1:T(8,128)}) %all-reduce.11.cloned.1.call-update) | async-done | bytes 106512 | tf_op jit(solution)/shard_map/psum | solution.py:51
  929.9 1.0 add_convert_fusion
  930.9 0.2 convolution_bitcast_fusion
  931.1 0.2 convolution_bitcast_fusion.1
  931.3 0.1 fusion.23
  931.4 0.1 pad_maximum_fusion
  931.5 0.7 copy.35
  (22 shorter events, 0.1 us)
Async XLA Ops:
  6.5 8.5 copy-start
  6.5 15.0 %copy-start.7 = (s32[4,4]{1,0:T(4,128)S(1)}, s32[4,4]{1,0:T(4,128)}, u32[]{:S(2)}) copy-start(s32[4,4]{1,0:T(4,128)} %param.13) | copy-start | bytes 196
  6.5 180.7 %all-gather.2.cloned.1.call-start = ((), (), s32[]{:S(2)}) async-start(), calls=%async_computation | async-start | bytes 14277120 | tf_op jit(solution)/shard_map/all_gather | solution.py:84
  8.7 394.1 %all-reduce.5.cloned.1.call-start = ((), (), s32[]{:S(2)}) async-start(), calls=%async_computation.1 | async-start | bytes 262144 | tf_op jit(solution)/shard_map/psum | solution.py:51
  230.4 16.0 %copy-start.1 = (bf16[2,8,4,16640]{3,1,2,0:T(8,128)(2,1)S(1)}, bf16[2,8,4,16640]{3,1,2,0:T(8,128)(2,1)}, u32[]{:S(2)}) copy-start(bf16[2,8,4,16640]{3,1,2,0:T(8,128)(2,1)} %convert_element_type.131) | copy-start | bytes 6389764
  252.3 326.1 %all-reduce.7.cloned.1.call-start = ((), (), s32[]{:S(2)}) async-start(), calls=%async_computation.2 | async-start | bytes 262144 | tf_op jit(solution)/shard_map/psum | solution.py:51
  415.4 338.7 %all-reduce.9.cloned.1.call-start = ((), (), s32[]{:S(2)}) async-start(), calls=%async_computation.3 | async-start | bytes 262144 | tf_op jit(solution)/shard_map/psum | solution.py:51
  591.2 338.7 %all-reduce.11.cloned.1.call-start = ((), (), s32[]{:S(2)}) async-start(), calls=%async_computation.4 | async-start | bytes 262144 | tf_op jit(solution)/shard_map/psum | solution.py:51
  760.3 6.6 copy-start.4
  760.3 169.7 %copy-start.2 = (f32[8,4,4,208]{3,0,2,1:T(8,128)S(1)}, f32[8,4,4,208]{3,0,2,1:T(8,128)}, u32[]{:S(2)}) copy-start(f32[8,4,4,208]{3,0,2,1:T(8,128)} %all-reduce.7.cloned.1.call-done) | copy-start | bytes 319492
  760.3 169.7 %copy-start.3 = (f32[8,4,4,208]{3,0,2,1:T(8,128)S(1)}, f32[8,4,4,208]{3,0,2,1:T(8,128)}, u32[]{:S(2)}) copy-start(f32[8,4,4,208]{3,0,2,1:T(8,128)} %all-reduce.9.cloned.1.call-done) | copy-start | bytes 319492
  760.3 169.7 %copy-start.5 = (f32[8,4,4,208]{3,0,2,1:T(8,128)S(1)}, f32[8,4,4,208]{3,0,2,1:T(8,128)}, u32[]{:S(2)}) copy-start(f32[8,4,4,208]{3,0,2,1:T(8,128)} %all-reduce.5.cloned.1.call-done) | copy-start | bytes 319492
  760.3 169.7 %copy-start.6 = (bf16[8,4,4,208]{3,2,1,0:T(4,128)(2,1)S(1)}, bf16[8,4,4,208]{3,2,1,0:T(4,128)(2,1)}, u32[]{:S(2)}) copy-start(bf16[8,4,4,208]{3,2,1,0:T(4,128)(2,1)} %param.8) | copy-start | bytes 159748
Sparse Core Ops, SparseCore 0:
  10.7 176.5 all-gather.1
  252.4 150.3 all-reduce.4
  415.5 162.8 all-reduce.6
  591.3 162.6 all-reduce.8
  767.0 162.8 all-reduce.10
where the time goes:
time: 948 us; the launch traced here: 939 us
  waiting for transfers between devices  803 us (85%)
  other arithmetic  56.3 us (6%)
  local copies, waits for them, and re-layouts  39.2 us (4%)
  matrix products  22.2 us (2%)
  between operations  17.4 us (2%)
    psum x4, waiting for transfers between devices, combine_blocks(): return lax.psum(by_target, 'pb')  639 us
    all_gather x1, waiting for transfers between devices, shards(): stored = lax.all_gather(chol, 'walk', axis=1, tiled=True)  164 us
    all_gather x1, other arithmetic, shards(): stored = lax.all_gather(chol, 'walk', axis=1, tiled=True)  43.1 us
    dot_general x4, matrix products, contract_slab(): jnp.einsum('prk,pkd->prd', weighted, matrix, preferred_element_type=jnp.f...  21.8 us
  transfers between devices with their start and end apart: 5, of which 5 were waited for; matrix products, arithmetic and copies ran while one was open for 1% of the time, Pallas kernels for 0%

commit v1 on v0

v1 whole, which is shorter than its diff:
```python
import jax
import jax.numpy as jnp
from jax import lax
from jax.experimental import pallas as pl
from jax.experimental.pallas import tpu as pltpu
from jax.sharding import PartitionSpec as P

ORDER = 4
NORB = 104
TILES = 11
PER = 5
MESH = pl.DeviceIdType.MESH
F32, BF16 = jnp.float32, jnp.bfloat16


def place():
    walk, pb = lax.axis_index("walk"), lax.axis_index("pb")
    return walk, pb, walk // 2, lax.rem(walk, 2)


def moved(site, step):
    z = lax.rem(site // 2 + lax.rem(step, 8), 8)
    return z * 2 + lax.rem(lax.rem(site, 2) + step // 8, 2)


def tile_of(site, pb):
    spot = lax.rem(lax.rem(site, 2) * 8 + site // 2 + 2 * (pb // 4) + lax.rem(pb, 4), 16)
    return spot - (spot + 1) // 3, lax.rem(spot, 3) != 1


def lanes_of(shape):
    return lax.broadcasted_iota(jnp.int32, shape, len(shape) - 1)


def unflatten(ref, lead, mats, rows):
    for a in range(13):
        x = (ref[0, :, a * 1664 : (a + 1) * 1664] if lead else ref[:, a * 1664 : (a + 1) * 1664]).astype(F32)
        y = jnp.stack([x[:, 208 * i : 208 * (i + 1)] for i in range(8)], axis=0)
        mats[:, 8 * a : 8 * a + 8, 0:208] = jnp.transpose(y, (1, 0, 2))


def pack(mats, packed):
    lanes = lanes_of((16, 128))
    for g in range(PER):
        for b in range(6):
            packed[b, g] = mats[g, 16 * b : 16 * b + 16, 0:128].astype(BF16)
        tail = jnp.where(lanes[:8] < 64, mats[g, 96:104, 128:256], 0.0)
        packed[6, g] = jnp.concatenate([mats[g, 96:104, 0:128], tail], axis=0).astype(BF16)
        for m in range(3):
            even = mats[g, 32 * m : 32 * m + 16, 128:256]
            odd = mats[g, 32 * m + 16 : 32 * m + 32, 128:256]
            packed[7 + m, g] = jnp.where(lanes < 64, even, pltpu.roll(odd, 64, 1)).astype(BF16)
        last = jnp.zeros((16, 128), F32)
        for b in range(7):
            block = mats[g, 16 * b : 16 * b + 16, 128:256]
            if b == 6:
                block = jnp.where(lax.broadcasted_iota(jnp.int32, (16, 128), 0) < 8, block, 0.0)
            block = pltpu.roll(block, (16 * b - 64) % 128, 1)
            last = jnp.where((lanes >= 16 * b) & (lanes < 16 * b + 16), block, last)
        packed[10, g] = last.astype(BF16)


def unpack(hr, right, j):
    lanes = lanes_of((16, 128))
    last = hr[j * TILES + 10].astype(F32)
    for b in range(7):
        if b < 6:
            block = hr[j * TILES + 7 + b // 2].astype(F32)
            if b % 2:
                block = pltpu.roll(block, 64, 1)
        else:
            block = hr[j * TILES + 6].astype(F32)
            block = jnp.concatenate([block[8:16], jnp.zeros((8, 128), F32)], axis=0)
        end = pltpu.roll(last, (64 - 16 * b) % 128, 1)
        block = jnp.where(lanes < 64, block, jnp.where(lanes < 80, end, 0.0))
        right[j, 16 * b : 16 * b + 16] = block.astype(BF16)
    right[j, 112:128] = jnp.zeros((16, 128), BF16)


def complex_join(acc):
    keep = lanes_of((16, 128)) < NORB
    low, high = acc[:, 0:128], acc[:, 104:232]
    real = jnp.where(keep, low[0:16] - high[16:32], 0.0)
    imag = jnp.where(keep, high[0:16] + low[16:32], 0.0)
    return jnp.concatenate([real, imag], axis=0)


def kernel(
    chol, ftile, start, spread, one_body, out,
    mats, obm, packed, crecv, cmat, plain, hs, hr, right, obuf,
    csend, crec, fsend, frec, hsend, hrec, hloc, osend, orec, ready,
):
    walk, pb, site, core = place()
    tile, maker = tile_of(site, pb)
    active = pb // 8 == core
    mine = lax.rem(pb, 8)

    def remote(src, dst, send, rec, to_walk, to_pb):
        return pltpu.make_async_remote_copy(
            src_ref=src, dst_ref=dst, send_sem=send, recv_sem=rec,
            device_id=(to_walk, to_pb), device_id_type=MESH,
        )

    barrier = pltpu.get_barrier_semaphore()
    sibling = walk + 1 - 2 * core
    for i in range(1, 16):
        pl.semaphore_signal(barrier, inc=1, device_id=(moved(site, i) * 2 + core, pb), device_id_type=MESH)
        pl.semaphore_signal(barrier, inc=1, device_id=(walk, lax.rem(pb + i, 16)), device_id_type=MESH)
    pl.semaphore_signal(barrier, inc=1, device_id=(sibling, pb), device_id_type=MESH)

    unflatten(chol, True, mats, PER)
    pack(mats, packed)
    for t in range(TILES):
        packed[t, PER] = ftile[...]

    pl.semaphore_wait(barrier, 31)
    for i in range(1, 16):
        pl.semaphore_signal(ready, inc=1, device_id=(walk, lax.rem(pb + i, 16)), device_id_type=MESH)

    for i in range(1, 16):
        there = moved(site, i)
        t, makes = tile_of(there, pb)

        @pl.when(makes)
        def _():
            remote(packed.at[t], crecv.at[site], csend, crec, there * 2 + core, pb).start()

    @pl.when(maker)
    def _():
        crecv[site] = packed[tile]

    unflatten(one_body, False, obm, 4)
    pl.semaphore_wait(ready, 15)

    @pl.when(maker)
    def _():
        remote(packed.at[0:10], packed.at[0:10], csend, crec, sibling, pb).wait_send()
        remote(crecv.at[0:15], crecv.at[0:15], csend, crec, sibling, pb).wait_recv()
        for kg in range(5):
            block = jnp.stack([crecv[(16 * kg + i) // PER, (16 * kg + i) % PER].astype(F32) for i in range(16)], axis=0)
            block = jnp.transpose(block, (1, 0, 2)).astype(BF16)
            cmat[:, pl.ds(pl.multiple_of(core * 80 + 16 * kg, 16), 16), :] = block
        half = cmat.at[:, pl.ds(pl.multiple_of(core * 80, 16), 80), :]
        copy = remote(half, half, fsend, frec, sibling, pb)
        copy.start()
        ft = crecv[:, PER].astype(F32)
        f = jnp.concatenate([ft[:, 0:8].reshape(128, 128), ft[:, 8:16].reshape(128, 128)[:, 0:32]], axis=1).astype(BF16)
        copy.wait()
        for p in range(0, 16, 2):
            rhs = jnp.concatenate([cmat[p], cmat[p + 1]], axis=1)
            both = jnp.dot(f, rhs, preferred_element_type=F32)
            plain[p] = both[:, 0:128]
            plain[p + 1] = both[:, 128:256]

        def send(site_to, i_to):
            return remote(
                hs.at[site_to * 8 + i_to], hr.at[pb * TILES + tile], hsend, hrec, site_to * 2 + core, core * 8 + i_to
            )

        def lay(there):
            rows = pl.ds(pl.multiple_of(there * 8, 8), 8)
            hs[rows] = jnp.transpose(plain[:, rows, :], (1, 0, 2)).astype(BF16)

        lay(site)

        @pl.when(active)
        def _():
            pltpu.make_async_copy(hs.at[site * 8 + mine], hr.at[pb * TILES + tile], hloc).start()

        @pl.when(jnp.logical_not(active))
        def _():
            send(site, mine).start()

        for di in range(1, 8):
            send(site, lax.rem(mine + di, 8)).start()

        def block(step, carry):
            there = moved(site, step)
            lay(there)
            for di in range(8):
                send(there, lax.rem(mine + di, 8)).start()
            return carry

        lax.fori_loop(1, 16, block, 0)

        @pl.when(active)
        def _():
            pltpu.make_async_copy(hs.at[site * 8 + mine], hr.at[pb * TILES + tile], hloc).wait()
            remote(hs.at[0:127], hs.at[0:127], hsend, hrec, sibling, pb).wait_send()

        @pl.when(jnp.logical_not(active))
        def _():
            remote(hs, hs, hsend, hrec, sibling, pb).wait_send()

    @pl.when(jnp.logical_not(maker))
    def _():
        remote(packed, packed, csend, crec, sibling, pb).wait_send()

    @pl.when(active)
    def _():
        @pl.when(maker)
        def _():
            remote(hr.at[0:175], hr.at[0:175], hsend, hrec, sibling, pb).wait_recv()

        @pl.when(jnp.logical_not(maker))
        def _():
            remote(hr, hr, hsend, hrec, sibling, pb).wait_recv()

        for j in range(16):
            unpack(hr, right, j)
        current = start[...]
        summed = current.astype(F32)
        for n in range(1, ORDER + 1):
            lhs = jnp.dot(spread[...], current, preferred_element_type=F32).astype(BF16)
            acc = jnp.zeros((32, 256), F32)
            for j in range(0, 16, 2):
                mats2 = [
                    jnp.concatenate([hr[i * TILES : i * TILES + 8].reshape(128, 128), right[i]], axis=1)
                    for i in (j, j + 1)
                ]
                rows2 = jnp.concatenate([lhs[32 * j : 32 * j + 32], lhs[32 * j + 32 : 32 * j + 64]], axis=1)
                acc += jnp.dot(rows2, jnp.concatenate(mats2, axis=0), preferred_element_type=F32)
            scaled = complex_join(acc) / float(n)
            summed = summed + scaled
            current = scaled.astype(BF16)
        section = summed.astype(BF16)
        kpoint = lax.rem(lax.broadcasted_iota(jnp.int32, (32, NORB), 0), 16) // 4
        acc = jnp.zeros((32, 256), F32)
        for k in range(4):
            rows = jnp.where(kpoint == k, section[:, 0:NORB].astype(F32), 0.0).astype(BF16)
            acc += jnp.dot(rows, obm[k].astype(BF16), preferred_element_type=F32)
        joined = complex_join(acc)
        zero = jnp.zeros((16, 128), F32)
        wide = jnp.concatenate([joined[0:16], zero], axis=1)
        wide += pltpu.roll(jnp.concatenate([joined[16:32], zero], axis=1), NORB, 1)
        obuf[mine] = wide.astype(BF16)
        for i in range(1, 16):
            remote(obuf.at[mine], obuf.at[mine], osend, orec, walk, lax.rem(pb + i, 16)).start()
        remote(obuf.at[0:7], obuf.at[0:7], osend, orec, sibling, pb).wait_recv()
        remote(hs.at[0:30], hs.at[0:30], osend, orec, sibling, pb).wait_send()

    @pl.when(jnp.logical_not(active))
    def _():
        remote(obuf, obuf, osend, orec, sibling, pb).wait_recv()

    out[...] = obuf[:, :, 0 : 2 * NORB]


def shards(bras, fields, chol, one_body, pair_table, kpq_map):
    walkers, kpoints, occupied, doubled = bras.shape
    pb = lax.axis_index("pb")
    charge = lax.dynamic_index_in_dim(pair_table[:, 0], pb, keepdims=False)
    f = lax.dynamic_index_in_dim(fields[0], charge, axis=1, keepdims=False)
    f = f.reshape(walkers, 16, 2, PER).transpose(0, 2, 1, 3).reshape(walkers, 160).astype(BF16)
    ftile = jnp.concatenate([f[:, 0:128], jnp.pad(f[:, 128:160], ((0, 0), (0, 96)))], axis=0)
    bra = lax.dynamic_index_in_dim(bras, lax.rem(pb, 8), keepdims=False)
    bra = bra.reshape(16, 2, NORB).transpose(1, 0, 2).reshape(32, NORB)
    start = jnp.pad(bra, ((0, 0), (0, 128 - NORB)))
    levels = jnp.arange(kpoints, dtype=jnp.int32)
    from_hot = (pair_table[:, 1:2] == levels).astype(jnp.int32)
    charge_hot = (pair_table[:, 0:1] == levels).astype(jnp.int32)
    target = jnp.sum(charge_hot[:, :, None] * from_hot[:, None, :] * kpq_map[None], axis=(1, 2))
    to_hot = (target[:, None] == levels).astype(jnp.int32)
    hot = to_hot[:, :, None] * from_hot[:, None, :]
    row = jnp.arange(32)
    same = (row[:, None] // 16 == row[None, :] // 16) & (row[:, None] % 4 == row[None, :] % 4)
    kp = row % 16 // 4
    spread = jnp.where(same[None], jnp.take(jnp.take(hot, kp, axis=1), kp, axis=2), 0)
    spread = spread.reshape(512, 32).astype(BF16)

    vmem = pl.BlockSpec(memory_space=pltpu.VMEM)
    dma = pltpu.SemaphoreType.DMA(())
    new = pl.pallas_call(
        kernel,
        out_shape=jax.ShapeDtypeStruct((walkers, 16, doubled), BF16),
        in_specs=[vmem] * 5,
        out_specs=vmem,
        scratch_shapes=[
            pltpu.VMEM((PER, 112, 256), F32),
            pltpu.VMEM((4, NORB, 256), F32),
            pltpu.VMEM((TILES, PER + 1, 16, 128), BF16),
            pltpu.VMEM((16, PER + 1, 16, 128), BF16),
            pltpu.VMEM((16, 160, 128), BF16),
            pltpu.VMEM((16, 128, 128), F32),
            pltpu.VMEM((128, 16, 128), BF16),
            pltpu.VMEM((16 * TILES, 16, 128), BF16),
            pltpu.VMEM((16, 128, 128), BF16),
            pltpu.VMEM((8, 16, 256), BF16),
            *[dma] * 9,
            pltpu.SemaphoreType.REGULAR,
        ],
        compiler_params=pltpu.CompilerParams(
            collective_id=0, has_side_effects=True, vmem_limit_bytes=32 * 2**20
        ),
        cost_estimate=pl.CostEstimate(flops=10**8, bytes_accessed=10**6, transcendentals=0),
    )(chol, ftile, start, spread, one_body)
    return new.reshape(walkers, kpoints, occupied, doubled)


def solution(mesh):
    return jax.shard_map(
        shards,
        mesh=mesh,
        in_specs=(
            P("walk", None, None, None),
            P(None, "walk", None, None),
            P("pb", "walk", None),
            P(),
            P(),
            P(),
        ),
        out_specs=P("walk", None, None, None),
        check_vma=False,
    )
```

time: 948 us -> 62.4 us (0.07)
  waiting for transfers between devices: 803 us -> 0 us
  other arithmetic: 56.3 us -> 0.37 us
  Pallas kernels: 0 us -> 53.5 us
  local copies, waits for them, and re-layouts: 39.2 us -> 6.19 us
  matrix products: 22.2 us -> 0 us
  between operations: 17.4 us -> 2.09 us
    psum x4 -> x0, waiting for transfers between devices: 639 us -> none  [combine_blocks(): return lax.psum(by_target, 'pb')]
    all_gather x1 -> x0, waiting for transfers between devices: 164 us -> none  [shards(): stored = lax.all_gather(chol, 'walk', axis=1, tiled=True)]
    pallas_call x0 -> x1, Pallas kernels: none -> 53.5 us  [shards(): pl.pallas_call(kernel, out_shape=jax.ShapeDtypeStruct((walkers, 16, doubl...]
    all_gather x1 -> x0, other arithmetic: 43.1 us -> none  [shards(): stored = lax.all_gather(chol, 'walk', axis=1, tiled=True)]
    dot_general x6 -> x0, matrix products: 22.2 us -> none  [the longest x4 21.8 us: contract_slab(): jnp.einsum('prk,pkd->prd', weighted, matrix, preferred_element_type=jnp.f...]
    convert_element_type x4, local copies, waits for them, and re-layouts: 18.2 us -> 1.09 us  [shards(): f.reshape(walkers, 16, 2, PER).transpose(0, 2, 1, 3).reshape(walkers, 160)]
    another operation x2 -> x0, local copies, waits for them, and re-layouts: 16 us -> none
  transfers between devices with their start and end apart: 5 -> 0, of which waited for: 5 -> 0; matrix products, arithmetic and copies ran while one was open for 1% -> 0% of each run, Pallas kernels for 0% -> 0%
where the time goes in v1:
time: 62.4 us; the launch traced here: 62.1 us
  Pallas kernels  53.5 us (86%)
  local copies, waits for them, and re-layouts  6.19 us (10%)
  between operations  2.09 us (3%)
    pallas_call x1, Pallas kernels, shards(): pl.pallas_call(kernel, out_shape=jax.ShapeDtypeStruct((walkers, 16, doubl...  53.5 us
    unnamed x10, local copies, waits for them, and re-layouts  2.29 us

profile of v1, /device:TPU:1, one launch (start us, length us, event | category | flops | bytes accessed | tf_op | source)
XLA Modules:
  0.0 62.1 jit_solution(7644400656216413213)
XLA Ops:
  0.0 0.0 copy-start
  0.0 0.0 copy-start.4
  0.0 0.7 %copy-done.4 = s32[16,2]{0,1:T(2,128)S(1)} copy-done((s32[16,2]{0,1:T(2,128)S(1)}, s32[16,2]{0,1:T(2,128)}, u32[]{:S(2)}) %copy-start.4) | copy-done | bytes 152
  0.7 0.6 constant_dynamic-slice_fusion.1
  3.2 0.8 %convert_reduce_fusion = bf16[8,160]{1,0:T(8,128)(2,1)S(1)} fusion(f32[1,8,4,160]{3,2,1,0:T(4,128)} %param.7, s32[]{:T(128)S(6)} %select_n.128), kind=kLoop, calls=%fused_computation.9 | loop fusion | bytes 5124 | tf_op jit(solution)/shard_map/convert_element_type | solution.py:254
  4.0 0.2 convert_element_type.41
  4.2 0.1 convert_element_type.43
  4.4 0.0 copy-done
  4.4 0.1 reshape.327
  4.5 0.0 copy-start.3
  4.5 0.7 %copy-done.3 = s32[4,4]{1,0:T(4,128)S(1)} copy-done((s32[4,4]{1,0:T(4,128)S(1)}, s32[4,4]{1,0:T(4,128)}, u32[]{:S(2)}) %copy-start.3) | copy-done | bytes 88
  5.2 0.1 multiply_reduce_fusion
  5.4 0.6 gather_fusion
  6.0 0.1 select_bitcast_fusion
  6.1 0.1 copy.10
  6.2 0.6 gather_fusion.1
  6.8 0.0 copy-start.1
  6.8 0.2 copy.11
  7.0 0.1 compare_and_fusion
  7.0 0.0 copy-start.2
  7.1 0.7 %copy-done.1 = bf16[1,5,21632]{2,1,0:T(8,128)(2,1)S(1)} copy-done((bf16[1,5,21632]{2,1,0:T(8,128)(2,1)S(1)}, bf16[1,5,21632]{2,1,0:T(8,128)(2,1)}, u32[]{:S(2)}) %copy-start.1) | copy-done | bytes 216344
  7.8 0.2 copy-done.2
  8.0 53.5 %shard_map.64 = bf16[8,16,208]{2,1,0:T(8,128)(2,1)S(1)} custom-call(bf16[1,5,21632]{2,1,0:T(8,128)(2,1)S(1)} %copy-done.1, bf16[16,128]{1,0:T(8,128)(2,1)S(1)} %fusion.3.ftile, bf16[32,128]{1,0:T(8,128)(2,1)S(1)} %pad.9.start, bf16[512,32]{1,0:T(8,128)(2,1)S(1)} %fusion.1.spread, bf16[4,21632]{1,0:T(4,128)(2,1)S(1)} %copy-done.2), custom_call_target="tpu_custom_call" | custom-call | flops 100000000 | bytes 1000000 | tf_op jit(solution)/shard_map/pallas_call | solution.py:273
  61.4 0.7 %reshape.329 = bf16[8,4,4,208]{3,2,1,0:T(4,128)(2,1)} reshape(bf16[8,16,208]{2,1,0:T(8,128)(2,1)S(1)} %shard_map.64) | data formatting | bytes 106496 | tf_op jit(solution)/shard_map/reshape | solution.py:297
  (16 shorter events, 0.2 us)
Async XLA Ops:
  0.0 4.4 %copy-start = (bf16[8,4,4,208]{3,2,1,0:T(4,128)(2,1)S(1)}, bf16[8,4,4,208]{3,2,1,0:T(4,128)(2,1)}, u32[]{:S(2)}) copy-start(bf16[8,4,4,208]{3,2,1,0:T(4,128)(2,1)} %param.6) | copy-start | bytes 159748
  0.0 0.7 %copy-start.4 = (s32[16,2]{0,1:T(2,128)S(1)}, s32[16,2]{0,1:T(2,128)}, u32[]{:S(2)}) copy-start(s32[16,2]{0,1:T(2,128)} %param.10) | copy-start | bytes 388
  4.5 0.7 %copy-start.3 = (s32[4,4]{1,0:T(4,128)S(1)}, s32[4,4]{1,0:T(4,128)}, u32[]{:S(2)}) copy-start(s32[4,4]{1,0:T(4,128)} %param.11) | copy-start | bytes 196
  6.8 1.0 %copy-start.1 = (bf16[1,5,21632]{2,1,0:T(8,128)(2,1)S(1)}, bf16[1,5,21632]{2,1,0:T(8,128)(2,1)}, u32[]{:S(2)}) copy-start(bf16[1,5,21632]{2,1,0:T(8,128)(2,1)} %chol.1) | copy-start | bytes 648964
  7.0 0.9 %copy-start.2 = (bf16[4,21632]{1,0:T(4,128)(2,1)S(1)}, bf16[4,21632]{1,0:T(4,128)(2,1)}, u32[]{:S(2)}) copy-start(bf16[4,21632]{1,0:T(4,128)(2,1)} %one_body.1) | copy-start | bytes 519172

commit v2 on v1

v2 whole, which is shorter than its diff:
```python
import jax
import jax.numpy as jnp
from jax import lax
from jax.experimental import pallas as pl
from jax.experimental.pallas import tpu as pltpu
from jax.sharding import PartitionSpec as P

ORDER = 4
NORB = 104
TILES = 11
PER = 5
FAR = (12, 11, 13, 4, 10, 14, 3, 5, 9, 15, 2, 6, 8, 1, 7, 0)
ORDER_SITES = (0, 2, 1, 4, 3, 6, 5, 8, 7, 10, 12, 14, 9, 11, 13, 15)
MESH = pl.DeviceIdType.MESH
F32, BF16 = jnp.float32, jnp.bfloat16


def place():
    walk, pb = lax.axis_index("walk"), lax.axis_index("pb")
    return walk, pb, walk // 2, lax.rem(walk, 2)


def moved(site, step):
    z = lax.rem(site // 2 + lax.rem(step, 8), 8)
    return z * 2 + lax.rem(lax.rem(site, 2) + step // 8, 2)


def tile_of(site, pb):
    spot = lax.rem(lax.rem(site, 2) * 8 + site // 2 + 2 * (pb // 4) + lax.rem(pb, 4), 16)
    return spot - (spot + 1) // 3, lax.rem(spot, 3) != 1, lax.rem(site // 2 + pb, 2)


def lanes_of(shape):
    return lax.broadcasted_iota(jnp.int32, shape, len(shape) - 1)


def unflatten(ref, lead, mats, rows):
    for a in range(13):
        x = (ref[0, :, a * 1664 : (a + 1) * 1664] if lead else ref[:, a * 1664 : (a + 1) * 1664]).astype(F32)
        y = jnp.stack([x[:, 208 * i : 208 * (i + 1)] for i in range(8)], axis=0)
        mats[:, 8 * a : 8 * a + 8, 0:208] = jnp.transpose(y, (1, 0, 2))


def pack(mats, packed):
    lanes = lanes_of((16, 128))
    for g in range(PER):
        for b in range(6):
            packed[b, g] = mats[g, 16 * b : 16 * b + 16, 0:128].astype(BF16)
        tail = jnp.where(lanes[:8] < 64, mats[g, 96:104, 128:256], 0.0)
        packed[6, g] = jnp.concatenate([mats[g, 96:104, 0:128], tail], axis=0).astype(BF16)
        for m in range(3):
            even = mats[g, 32 * m : 32 * m + 16, 128:256]
            odd = mats[g, 32 * m + 16 : 32 * m + 32, 128:256]
            packed[7 + m, g] = jnp.where(lanes < 64, even, pltpu.roll(odd, 64, 1)).astype(BF16)
        last = jnp.zeros((16, 128), F32)
        for b in range(7):
            block = mats[g, 16 * b : 16 * b + 16, 128:256]
            if b == 6:
                block = jnp.where(lax.broadcasted_iota(jnp.int32, (16, 128), 0) < 8, block, 0.0)
            block = pltpu.roll(block, (16 * b - 64) % 128, 1)
            last = jnp.where((lanes >= 16 * b) & (lanes < 16 * b + 16), block, last)
        packed[10, g] = last.astype(BF16)


def unpack(hr, right, j):
    lanes = lanes_of((16, 128))
    last = hr[j * TILES + 10].astype(F32)
    for b in range(7):
        if b < 6:
            block = hr[j * TILES + 7 + b // 2].astype(F32)
            if b % 2:
                block = pltpu.roll(block, 64, 1)
        else:
            block = hr[j * TILES + 6].astype(F32)
            block = jnp.concatenate([block[8:16], jnp.zeros((8, 128), F32)], axis=0)
        end = pltpu.roll(last, (64 - 16 * b) % 128, 1)
        block = jnp.where(lanes < 64, block, jnp.where(lanes < 80, end, 0.0))
        right[j, 16 * b : 16 * b + 16] = block.astype(BF16)
    right[j, 112:128] = jnp.zeros((16, 128), BF16)


def complex_join(acc):
    keep = lanes_of((16, 128)) < NORB
    low, high = acc[:, 0:128], acc[:, 104:232]
    real = jnp.where(keep, low[0:16] - high[16:32], 0.0)
    imag = jnp.where(keep, high[0:16] + low[16:32], 0.0)
    return jnp.concatenate([real, imag], axis=0)


def field_tile(fields, charge):
    f = jnp.zeros((8, 160), F32)
    for q in range(4):
        f = jnp.where(charge == q, fields[0, :, q, :], f)
    rest = jnp.concatenate([f[:, 128:160], jnp.zeros((8, 96), F32)], axis=1)
    return jnp.concatenate([f[:, 0:128], rest], axis=0).astype(BF16)


def spread_rows(pairs, kpq, spread):
    row = lax.broadcasted_iota(jnp.int32, (32, 32), 0)
    col = lax.broadcasted_iota(jnp.int32, (32, 32), 1)
    same = (row // 16 == col // 16) & (row % 4 == col % 4)
    row, col = row % 16 // 4, col % 16 // 4
    for j in range(16):
        source = pairs[1, j]
        target = kpq[pairs[0, j], source]
        spread[32 * j : 32 * j + 32] = jnp.where(same & (row == target) & (col == source), 1.0, 0.0).astype(BF16)


def split_rows(bras, mine):
    rows = jnp.concatenate([bras[mine, k].astype(F32) for k in range(4)], axis=0)
    wide = jnp.concatenate([rows, jnp.zeros((16, 48), F32)], axis=1)
    keep = lanes_of((16, 128)) < NORB
    halves = [jnp.where(keep, wide[:, 0:128], 0.0), jnp.where(keep, wide[:, NORB : NORB + 128], 0.0)]
    return jnp.concatenate(halves, axis=0)


def kernel(
    bras_in, fields_in, chol_in, one_body_in, pairs, kpq, out,
    bras, fields, chol, one_body, spread,
    mats, obm, packed, crecv, cmat, plain, hs, hr, right, obuf,
    load, csend, crec, hsend, hrec, hloc, osend, orec, ready,
):
    walk, pb, site, core = place()
    tile, makes, maker_core = tile_of(site, pb)
    maker = makes & (maker_core == core)
    active = pb // 8 != core
    mine = lax.rem(pb, 8)

    def remote(src, dst, send, rec, to_walk, to_pb):
        return pltpu.make_async_remote_copy(
            src_ref=src, dst_ref=dst, send_sem=send, recv_sem=rec,
            device_id=(to_walk, to_pb), device_id_type=MESH,
        )

    loads = [
        pltpu.make_async_copy(src, dst, load.at[i])
        for i, (src, dst) in enumerate([(chol_in, chol), (fields_in, fields), (one_body_in, one_body), (bras_in, bras)])
    ]
    for copy in loads:
        copy.start()
    barrier = pltpu.get_barrier_semaphore()
    sibling = walk + 1 - 2 * core
    for i in FAR:
        for c in (0, 1) if i else (1,):
            to = moved(site, i) * 2 + lax.rem(core + c, 2)
            pl.semaphore_signal(barrier, inc=1, device_id=(to, pb), device_id_type=MESH)
    for i in range(1, 16):
        pl.semaphore_signal(barrier, inc=1, device_id=(walk, lax.rem(pb + i, 16)), device_id_type=MESH)

    loads[0].wait()
    unflatten(chol, True, mats, PER)
    pack(mats, packed)
    loads[1].wait()
    ftile = field_tile(fields, pairs[0, pb])
    for t in range(TILES):
        packed[t, PER] = ftile

    pl.semaphore_wait(barrier, 46)
    for i in range(1, 16):
        pl.semaphore_signal(ready, inc=1, device_id=(walk, lax.rem(pb + i, 16)), device_id_type=MESH)

    for i in FAR:
        there = moved(site, i)
        t, used, c = tile_of(there, pb)

        @pl.when(used & ((c != core) if i == 0 else True))
        def _():
            remote(packed.at[t], crecv.at[walk], csend, crec, there * 2 + c, pb).start()

    @pl.when(maker)
    def _():
        crecv[walk] = packed[tile]

    loads[2].wait()
    unflatten(one_body, False, obm, 4)
    spread_rows(pairs, kpq, spread)
    loads[3].wait()
    pl.semaphore_wait(ready, 15)

    @pl.when(maker)
    def _():
        remote(crecv.at[0:31], crecv.at[0:31], csend, crec, sibling, pb).wait_recv()
        for kg in range(10):
            block = jnp.stack([crecv[(16 * kg + i) // PER, (16 * kg + i) % PER].astype(F32) for i in range(16)], axis=0)
            cmat[:, 16 * kg : 16 * kg + 16, :] = jnp.transpose(block, (1, 0, 2)).astype(BF16)
        ft = crecv[:, PER].astype(F32)
        f = jnp.concatenate([ft[:, 0:8].reshape(256, 128), ft[:, 8:16].reshape(256, 128)[:, 0:32]], axis=1).astype(BF16)
        for p in range(0, 16, 2):
            rhs = jnp.concatenate([cmat[p], cmat[p + 1]], axis=1)
            both = jnp.dot(f, rhs, preferred_element_type=F32)
            plain[p] = both[:, 0:128]
            plain[p + 1] = both[:, 128:256]

        def send(to, i):
            return remote(hs.at[to * 8 + i], hr.at[pb * TILES + tile], hsend, hrec, to, 8 - lax.rem(to, 2) * 8 + i)

        for to in range(32):
            hs[8 * to : 8 * to + 8] = jnp.transpose(plain[:, 8 * to : 8 * to + 8, :], (1, 0, 2)).astype(BF16)

        @pl.when(active)
        def _():
            pltpu.make_async_copy(hs.at[walk * 8 + mine], hr.at[pb * TILES + tile], hloc).start()

        for there in ORDER_SITES:
            for to in (2 * there, 2 * there + 1):

                @pl.when((to != walk) | jnp.logical_not(active))
                def _():
                    send(to, mine).start()

                def rest(di, carry):
                    send(to, lax.rem(mine + di, 8)).start()
                    return carry

                lax.fori_loop(1, 8, rest, 0)

    @pl.when(active)
    def _():
        @pl.when(maker)
        def _():
            pltpu.make_async_copy(hs.at[walk * 8 + mine], hr.at[pb * TILES + tile], hloc).wait()
            remote(hr.at[0:175], hr.at[0:175], hsend, hrec, sibling, pb).wait_recv()

        @pl.when(jnp.logical_not(maker))
        def _():
            remote(hr, hr, hsend, hrec, sibling, pb).wait_recv()

        for j in range(16):
            unpack(hr, right, j)
        summed = split_rows(bras, mine)
        current = summed.astype(BF16)
        for n in range(1, ORDER + 1):
            lhs = jnp.dot(spread[...], current, preferred_element_type=F32).astype(BF16)
            acc = jnp.zeros((32, 256), F32)
            for j in range(0, 16, 2):
                mats2 = [
                    jnp.concatenate([hr[i * TILES : i * TILES + 8].reshape(128, 128), right[i]], axis=1)
                    for i in (j, j + 1)
                ]
                rows2 = jnp.concatenate([lhs[32 * j : 32 * j + 32], lhs[32 * j + 32 : 32 * j + 64]], axis=1)
                acc += jnp.dot(rows2, jnp.concatenate(mats2, axis=0), preferred_element_type=F32)
            scaled = complex_join(acc) / float(n)
            summed = summed + scaled
            current = scaled.astype(BF16)
        section = summed.astype(BF16)
        kpoint = lax.rem(lax.broadcasted_iota(jnp.int32, (32, NORB), 0), 16) // 4
        acc = jnp.zeros((32, 256), F32)
        for k in range(4):
            rows = jnp.where(kpoint == k, section[:, 0:NORB].astype(F32), 0.0).astype(BF16)
            acc += jnp.dot(rows, obm[k].astype(BF16), preferred_element_type=F32)
        joined = complex_join(acc)
        zero = jnp.zeros((16, 128), F32)
        wide = jnp.concatenate([joined[0:16], zero], axis=1)
        wide += pltpu.roll(jnp.concatenate([joined[16:32], zero], axis=1), NORB, 1)
        obuf[mine] = wide.astype(BF16)
        for i in range(1, 16):
            remote(obuf.at[mine], obuf.at[mine], osend, orec, walk, lax.rem(pb + i, 16)).start()
        remote(obuf.at[0:7], obuf.at[0:7], osend, orec, sibling, pb).wait_recv()

    @pl.when(jnp.logical_not(active))
    def _():
        remote(obuf, obuf, osend, orec, sibling, pb).wait_recv()

    @pl.when(maker)
    def _():
        remote(packed.at[0:10], packed.at[0:10], csend, crec, sibling, pb).wait_send()

        @pl.when(active)
        def _():
            remote(hs.at[0:255], hs.at[0:255], hsend, hrec, sibling, pb).wait_send()

        @pl.when(jnp.logical_not(active))
        def _():
            remote(hs, hs, hsend, hrec, sibling, pb).wait_send()

    @pl.when(jnp.logical_not(maker))
    def _():
        remote(packed, packed, csend, crec, sibling, pb).wait_send()

    @pl.when(active)
    def _():
        remote(hs.at[0:30], hs.at[0:30], osend, orec, sibling, pb).wait_send()

    for w in range(8):
        rows = obuf[w].astype(F32)
        for k in range(4):
            out[w, k] = rows[4 * k : 4 * k + 4, 0 : 2 * NORB].astype(BF16)


def shards(bras, fields, chol, one_body, pair_table, kpq_map):
    anywhere, smem = pl.BlockSpec(memory_space=pltpu.HBM), pl.BlockSpec(memory_space=pltpu.SMEM)
    dma = pltpu.SemaphoreType.DMA(())
    return pl.pallas_call(
        kernel,
        out_shape=jax.ShapeDtypeStruct(bras.shape, BF16),
        in_specs=[anywhere] * 4 + [smem] * 2,
        out_specs=pl.BlockSpec(memory_space=pltpu.VMEM),
        scratch_shapes=[
            pltpu.VMEM(bras.shape, BF16),
            pltpu.VMEM(fields.shape, F32),
            pltpu.VMEM(chol.shape, BF16),
            pltpu.VMEM(one_body.shape, BF16),
            pltpu.VMEM((512, 32), BF16),
            pltpu.VMEM((PER, 112, 256), F32),
            pltpu.VMEM((4, NORB, 256), F32),
            pltpu.VMEM((TILES, PER + 1, 16, 128), BF16),
            pltpu.VMEM((32, PER + 1, 16, 128), BF16),
            pltpu.VMEM((16, 160, 128), BF16),
            pltpu.VMEM((16, 256, 128), F32),
            pltpu.VMEM((256, 16, 128), BF16),
            pltpu.VMEM((16 * TILES, 16, 128), BF16),
            pltpu.VMEM((16, 128, 128), BF16),
            pltpu.VMEM((8, 16, 256), BF16),
            pltpu.SemaphoreType.DMA((4,)),
            *[dma] * 7,
            pltpu.SemaphoreType.REGULAR,
        ],
        compiler_params=pltpu.CompilerParams(
            collective_id=0, has_side_effects=True, vmem_limit_bytes=60 * 2**20
        ),
        cost_estimate=pl.CostEstimate(flops=10**8, bytes_accessed=10**6, transcendentals=0),
    )(bras, fields, chol, one_body, pair_table.T, kpq_map)


def solution(mesh):
    return jax.shard_map(
        shards,
        mesh=mesh,
        in_specs=(
            P("walk", None, None, None),
            P(None, "walk", None, None),
            P("pb", "walk", None),
            P(),
            P(),
            P(),
        ),
        out_specs=P("walk", None, None, None),
        check_vma=False,
    )
```

time: 62.4 us -> 49.3 us (0.79)
  Pallas kernels: 53.5 us -> 47.5 us
  local copies, waits for them, and re-layouts: 6.19 us -> 1.49 us
  between operations: 2.09 us -> 0.01 us
    pallas_call x1, Pallas kernels: 53.5 us -> 47.5 us  [shards(): pl.pallas_call(kernel, out_shape=jax.ShapeDtypeStruct(bras.shape, BF16),...]
    gather x3 -> x0, local copies, waits for them, and re-layouts: 1.36 us -> none  [the longest x2 0.75 us: shards(): jnp.take(jnp.take(hot, kp, axis=1), kp, axis=2)]
    convert_element_type x4 -> x0, local copies, waits for them, and re-layouts: 1.09 us -> none  [shards(): f.reshape(walkers, 16, 2, PER).transpose(0, 2, 1, 3).reshape(walkers, 160)]
    unnamed x10 -> x1, local copies, waits for them, and re-layouts: 2.29 us -> 1.49 us
    reshape x2 -> x0, local copies, waits for them, and re-layouts: 0.74 us -> none  [the longest x1 0.65 us: shards(): return new.reshape(walkers, kpoints, occupied, doubled)]
where the time goes in v2:
time: 49.3 us; the launch traced here: 49 us
  Pallas kernels  47.5 us (96%)
  local copies, waits for them, and re-layouts  1.49 us (3%)
    pallas_call x1, Pallas kernels, shards(): pl.pallas_call(kernel, out_shape=jax.ShapeDtypeStruct(bras.shape, BF16),...  47.5 us
    unnamed x1, local copies, waits for them, and re-layouts  1.49 us

profile of v2, /device:TPU:1, one launch (start us, length us, event | category | flops | bytes accessed | tf_op | source)
XLA Modules:
  0.0 49.0 jit_solution(12415062956596828129)
XLA Ops:
  0.0 47.5 %shard_map.64 = bf16[8,4,4,208]{3,2,1,0:T(4,128)(2,1)} custom-call(bf16[8,4,4,208]{3,2,1,0:T(4,128)(2,1)} %bras_in.1, f32[1,8,4,160]{3,2,1,0:T(4,128)} %fields_in.1, bf16[1,5,21632]{2,1,0:T(8,128)(2,1)} %chol_in.1, bf16[4,21632]{1,0:T(4,128)(2,1)} %one_body_in.1, s32[2,16]{1,0:T(2,128)} %bitcast.1, s32[4,4]{1,0:T(4,128)} %kpq.1), custom_call_target="tpu_custom_call" | custom-call | flops 100000000 | bytes 1000000 | tf_op jit(solution)/shard_map/pallas_call | solution.py:293
  47.5 1.5 %copy.8 = bf16[8,4,4,208]{3,2,1,0:T(4,128)(2,1)} copy(bf16[8,4,4,208]{3,2,1,0:T(4,128)(2,1)} %shard_map.64) | data formatting | bytes 106496

commit v3 on v2

v3 whole, which is shorter than its diff:
```python
import jax
import jax.numpy as jnp
from jax import lax
from jax.experimental import pallas as pl
from jax.experimental.pallas import tpu as pltpu
from jax.sharding import PartitionSpec as P

ORDER = 4
NORB = 104
TILES = 11
PER = 5
FAR = (12, 11, 13, 4, 10, 14, 3, 5, 9, 15, 2, 6, 8, 1, 7, 0)
BLOCKS = ((0, 64, (0, 2, 1, 3)), (64, 256, (4, 6, 5, 8, 7, 10, 12, 14, 9, 11, 13, 15)))
MESH = pl.DeviceIdType.MESH
F32, BF16 = jnp.float32, jnp.bfloat16


def place():
    walk, pb = lax.axis_index("walk"), lax.axis_index("pb")
    return walk, pb, walk // 2, lax.rem(walk, 2)


def moved(site, step):
    z = lax.rem(site // 2 + lax.rem(step, 8), 8)
    return z * 2 + lax.rem(lax.rem(site, 2) + step // 8, 2)


def tile_of(site, pb):
    spot = lax.rem(lax.rem(site, 2) * 8 + site // 2 + 2 * (pb // 4) + lax.rem(pb, 4), 16)
    return spot - (spot + 1) // 3, lax.rem(spot, 3) != 1, lax.rem(site // 2 + pb, 2)


def lanes_of(shape):
    return lax.broadcasted_iota(jnp.int32, shape, len(shape) - 1)


def unflatten(ref, lead, mats, rows):
    for a in range(13):
        x = (ref[0, :, a * 1664 : (a + 1) * 1664] if lead else ref[:, a * 1664 : (a + 1) * 1664]).astype(F32)
        y = jnp.stack([x[:, 208 * i : 208 * (i + 1)] for i in range(8)], axis=0)
        mats[:, 8 * a : 8 * a + 8, 0:208] = jnp.transpose(y, (1, 0, 2))


def pack(mats, packed):
    lanes = lanes_of((16, 128))
    for g in range(PER):
        for b in range(6):
            packed[b, g] = mats[g, 16 * b : 16 * b + 16, 0:128].astype(BF16)
        tail = jnp.where(lanes[:8] < 64, mats[g, 96:104, 128:256], 0.0)
        packed[6, g] = jnp.concatenate([mats[g, 96:104, 0:128], tail], axis=0).astype(BF16)
        for m in range(3):
            even = mats[g, 32 * m : 32 * m + 16, 128:256]
            odd = mats[g, 32 * m + 16 : 32 * m + 32, 128:256]
            packed[7 + m, g] = jnp.where(lanes < 64, even, pltpu.roll(odd, 64, 1)).astype(BF16)
        last = jnp.zeros((16, 128), F32)
        for b in range(7):
            block = mats[g, 16 * b : 16 * b + 16, 128:256]
            if b == 6:
                block = jnp.where(lax.broadcasted_iota(jnp.int32, (16, 128), 0) < 8, block, 0.0)
            block = pltpu.roll(block, (16 * b - 64) % 128, 1)
            last = jnp.where((lanes >= 16 * b) & (lanes < 16 * b + 16), block, last)
        packed[10, g] = last.astype(BF16)


def unpack(hr, right, j):
    lanes = lanes_of((16, 128))
    last = hr[j * TILES + 10].astype(F32)
    for b in range(7):
        if b < 6:
            block = hr[j * TILES + 7 + b // 2].astype(F32)
            if b % 2:
                block = pltpu.roll(block, 64, 1)
        else:
            block = hr[j * TILES + 6].astype(F32)
            block = jnp.concatenate([block[8:16], jnp.zeros((8, 128), F32)], axis=0)
        end = pltpu.roll(last, (64 - 16 * b) % 128, 1)
        block = jnp.where(lanes < 64, block, jnp.where(lanes < 80, end, 0.0))
        right[j, 16 * b : 16 * b + 16] = block.astype(BF16)
    right[j, 112:128] = jnp.zeros((16, 128), BF16)


def complex_join(acc):
    keep = lanes_of((4, 128)) < NORB
    low, high = acc[:, 0:128], acc[:, NORB : NORB + 128]
    return jnp.where(keep, low[0:4] - high[4:8], 0.0), jnp.where(keep, high[0:4] + low[4:8], 0.0)


def as_rows(rows):
    return jnp.concatenate([rows, jnp.zeros((8, 128), F32)], axis=0).astype(BF16)


def field_tile(fields, charge):
    f = jnp.zeros((8, 160), F32)
    for q in range(4):
        f = jnp.where(charge == q, fields[0, :, q, :], f)
    rest = jnp.concatenate([f[:, 128:160], jnp.zeros((8, 96), F32)], axis=1)
    return jnp.concatenate([f[:, 0:128], rest], axis=0).astype(BF16)


def split_rows(bras, mine, k):
    wide = jnp.concatenate([bras[mine, k].astype(F32), jnp.zeros((4, 48), F32)], axis=1)
    keep = lanes_of((4, 128)) < NORB
    halves = [jnp.where(keep, wide[:, i : i + 128], 0.0) for i in (0, NORB)]
    return jnp.concatenate(halves, axis=0)


def kernel(
    bras_in, fields_in, chol_in, one_body_in, pairs_in, kpq_in, out,
    bras, fields, chol, one_body, pairs, kpq,
    mats, obm, propagator, packed, crecv, cmat, plain, hs, hr, right, current, obuf,
    load, hrec, csend, crec, hsend, hloc, osend, orec, ready,
):
    walk, pb, site, core = place()
    tile, makes, maker_core = tile_of(site, pb)
    maker = makes & (maker_core == core)
    active = pb // 8 != core
    mine = lax.rem(pb, 8)

    def remote(src, dst, send, rec, to_walk, to_pb):
        return pltpu.make_async_remote_copy(
            src_ref=src, dst_ref=dst, send_sem=send, recv_sem=rec,
            device_id=(to_walk, to_pb), device_id_type=MESH,
        )

    loads = [
        pltpu.make_async_copy(src, dst, load.at[i])
        for i, (src, dst) in enumerate(
            [(chol_in, chol), (fields_in, fields), (one_body_in, one_body)]
            + [(bras_in, bras), (pairs_in, pairs), (kpq_in, kpq)]
        )
    ]
    barrier = pltpu.get_barrier_semaphore()
    sibling = walk + 1 - 2 * core
    for i in FAR:
        for c in (0, 1) if i else (1,):
            to = moved(site, i) * 2 + lax.rem(core + c, 2)
            pl.semaphore_signal(barrier, inc=1, device_id=(to, pb), device_id_type=MESH)
    for i in range(1, 16):
        pl.semaphore_signal(barrier, inc=1, device_id=(walk, lax.rem(pb + i, 16)), device_id_type=MESH)

    for copy in loads:
        copy.start()
    loads[0].wait()
    unflatten(chol, True, mats, PER)
    pack(mats, packed)
    loads[1].wait()
    loads[4].wait()
    ftile = field_tile(fields, pairs[0, pb])
    for t in range(TILES):
        packed[t, PER] = ftile

    hands = []
    for i in FAR:
        there = moved(site, i)
        t, used, c = tile_of(there, pb)
        hands.append((there, t, used & (c != core) if i == 0 else used, c))
    pl.semaphore_wait(barrier, 46)
    for i in range(1, 16):
        pl.semaphore_signal(ready, inc=1, device_id=(walk, lax.rem(pb + i, 16)), device_id_type=MESH)

    for there, t, used, c in hands:

        @pl.when(used)
        def _():
            remote(packed.at[t], crecv.at[walk], csend, crec, there * 2 + c, pb).start()

    @pl.when(maker)
    def _():
        crecv[walk] = packed[tile]

    loads[2].wait()
    unflatten(one_body, False, obm, 4)
    for k in range(4):
        obm[k, NORB:112] = jnp.zeros((8, 256), F32)
        propagator[k, 0:112] = obm[k].astype(BF16)
        propagator[k, 112:128] = jnp.zeros((16, 256), BF16)
    loads[3].wait()
    loads[5].wait()
    pl.semaphore_wait(ready, 15)

    @pl.when(maker)
    def _():
        remote(crecv.at[0:31], crecv.at[0:31], csend, crec, sibling, pb).wait_recv()
        for kg in range(10):
            block = jnp.stack([crecv[(16 * kg + i) // PER, (16 * kg + i) % PER].astype(F32) for i in range(16)], axis=0)
            cmat[:, 16 * kg : 16 * kg + 16, :] = jnp.transpose(block, (1, 0, 2)).astype(BF16)
        ft = crecv[:, PER].astype(F32)
        f = jnp.concatenate([ft[:, 0:8].reshape(256, 128), ft[:, 8:16].reshape(256, 128)[:, 0:32]], axis=1).astype(BF16)
        def send(to, i):
            return remote(hs.at[to * 8 + i], hr.at[pb * TILES + tile], hsend, hrec.at[pb // 4], to, 8 - lax.rem(to, 2) * 8 + i)

        for start, stop, sites in BLOCKS:
            for p in range(0, 16, 2):
                rhs = jnp.concatenate([cmat[p], cmat[p + 1]], axis=1)
                both = jnp.dot(f[start:stop], rhs, preferred_element_type=F32)
                plain[p, start:stop] = both[:, 0:128]
                plain[p + 1, start:stop] = both[:, 128:256]
            for to in range(start // 8, stop // 8):
                hs[8 * to : 8 * to + 8] = jnp.transpose(plain[:, 8 * to : 8 * to + 8, :], (1, 0, 2)).astype(BF16)
            for there in sites:
                for to in (2 * there, 2 * there + 1):

                    @pl.when((to != walk) | jnp.logical_not(active))
                    def _():
                        send(to, mine).start()

                    def rest(di, carry):
                        send(to, lax.rem(mine + di, 8)).start()
                        return carry

                    lax.fori_loop(1, 8, rest, 0)

        @pl.when(active)
        def _():
            pltpu.make_async_copy(hs.at[walk * 8 + mine], hr.at[pb * TILES + tile], hloc).start()

    @pl.when(active)
    def _():
        sources = [pairs[1, j] for j in range(16)]
        targets = [kpq[pairs[0, j], sources[j]] for j in range(16)]
        summed = [split_rows(bras, mine, k) for k in range(4)]
        for k in range(4):
            current[k] = as_rows(summed[k])

        def arrived(group, ones):
            some = hr.at[pl.ds(group * 4 * TILES, ones)]
            return remote(some, some, hsend, hrec.at[group], sibling, pb)

        @pl.when(maker)
        def _():
            pltpu.make_async_copy(hs.at[walk * 8 + mine], hr.at[pb * TILES + tile], hloc).wait()

        for n in range(1, ORDER + 1):
            acc = [jnp.zeros((8, 256), F32) for _ in range(4)]
            for j in range(16):
                if n == 1 and j % 4 == 0:
                    own = maker & (pb // 4 == j // 4)

                    @pl.when(own)
                    def _():
                        arrived(j // 4, 4 * TILES - 1).wait_recv()

                    @pl.when(jnp.logical_not(own))
                    def _():
                        arrived(j // 4, 4 * TILES).wait_recv()

                if n == 1:
                    unpack(hr, right, j)
                matrix = jnp.concatenate([hr[j * TILES : j * TILES + 8].reshape(128, 128), right[j]], axis=1)
                product = jnp.dot(current[sources[j]], matrix, preferred_element_type=F32)[0:8]
                acc = [acc[k] + jnp.where(targets[j] == k, product, 0.0) for k in range(4)]
            for k in range(4):
                scaled = jnp.concatenate(complex_join(acc[k]), axis=0) * (1.0 / n)
                summed[k] = summed[k] + scaled
                current[k] = as_rows(scaled)
        joined = [
            complex_join(jnp.dot(as_rows(summed[k]), propagator[k], preferred_element_type=F32)) for k in range(4)
        ]
        real, imag = (jnp.concatenate([one[i] for one in joined], axis=0) for i in (0, 1))
        zero = jnp.zeros((16, 128), F32)
        wide = jnp.concatenate([real, zero], axis=1)
        wide += pltpu.roll(jnp.concatenate([imag, zero], axis=1), NORB, 1)
        obuf[mine] = wide.astype(BF16)
        for i in range(1, 16):
            remote(obuf.at[mine], obuf.at[mine], osend, orec, walk, lax.rem(pb + i, 16)).start()
        remote(obuf.at[0:7], obuf.at[0:7], osend, orec, sibling, pb).wait_recv()

    @pl.when(jnp.logical_not(active))
    def _():
        remote(obuf, obuf, osend, orec, sibling, pb).wait_recv()

    @pl.when(maker)
    def _():
        remote(packed.at[0:10], packed.at[0:10], csend, crec, sibling, pb).wait_send()

        @pl.when(active)
        def _():
            remote(hs.at[0:255], hs.at[0:255], hsend, hrec.at[0], sibling, pb).wait_send()

        @pl.when(jnp.logical_not(active))
        def _():
            remote(hs, hs, hsend, hrec.at[0], sibling, pb).wait_send()

    @pl.when(jnp.logical_not(maker))
    def _():
        remote(packed, packed, csend, crec, sibling, pb).wait_send()

    @pl.when(active)
    def _():
        remote(hs.at[0:30], hs.at[0:30], osend, orec, sibling, pb).wait_send()

    for w in range(8):
        rows = obuf[w].astype(F32)
        for k in range(4):
            out[w, k] = rows[4 * k : 4 * k + 4, 0 : 2 * NORB].astype(BF16)


def shards(bras, fields, chol, one_body, pair_table, kpq_map):
    dma = pltpu.SemaphoreType.DMA(())
    return pl.pallas_call(
        kernel,
        out_shape=jax.ShapeDtypeStruct(bras.shape, BF16),
        in_specs=[pl.BlockSpec(memory_space=pltpu.HBM)] * 6,
        out_specs=pl.BlockSpec(memory_space=pltpu.VMEM),
        scratch_shapes=[
            pltpu.VMEM(bras.shape, BF16),
            pltpu.VMEM(fields.shape, F32),
            pltpu.VMEM(chol.shape, BF16),
            pltpu.VMEM(one_body.shape, BF16),
            pltpu.SMEM((2, 16), jnp.int32),
            pltpu.SMEM((4, 4), jnp.int32),
            pltpu.VMEM((PER, 112, 256), F32),
            pltpu.VMEM((4, 112, 256), F32),
            pltpu.VMEM((4, 128, 256), BF16),
            pltpu.VMEM((TILES, PER + 1, 16, 128), BF16),
            pltpu.VMEM((32, PER + 1, 16, 128), BF16),
            pltpu.VMEM((16, 160, 128), BF16),
            pltpu.VMEM((16, 256, 128), F32),
            pltpu.VMEM((256, 16, 128), BF16),
            pltpu.VMEM((16 * TILES, 16, 128), BF16),
            pltpu.VMEM((16, 128, 128), BF16),
            pltpu.VMEM((4, 16, 128), BF16),
            pltpu.VMEM((8, 16, 256), BF16),
            pltpu.SemaphoreType.DMA((6,)),
            pltpu.SemaphoreType.DMA((4,)),
            *[dma] * 6,
            pltpu.SemaphoreType.REGULAR,
        ],
        compiler_params=pltpu.CompilerParams(
            collective_id=0, has_side_effects=True, vmem_limit_bytes=60 * 2**20
        ),
        cost_estimate=pl.CostEstimate(flops=10**8, bytes_accessed=10**6, transcendentals=0),
    )(bras, fields, chol, one_body, pair_table.T, kpq_map)


def solution(mesh):
    return jax.shard_map(
        shards,
        mesh=mesh,
        in_specs=(
            P("walk", None, None, None),
            P(None, "walk", None, None),
            P("pb", "walk", None),
            P(),
            P(),
            P(),
        ),
        out_specs=P("walk", None, None, None),
        check_vma=False,
    )
```

time: 49.3 us -> 47.9 us (0.972)
  Pallas kernels: 47.5 us -> 46.2 us
    pallas_call x1, Pallas kernels: 47.5 us -> 46.2 us  [shards(): pl.pallas_call(kernel, out_shape=jax.ShapeDtypeStruct(bras.shape, BF16),...]
where the time goes in v3:
time: 47.9 us; the launch traced here: 47.7 us
  Pallas kernels  46.2 us (96%)
  local copies, waits for them, and re-layouts  1.49 us (3%)
    pallas_call x1, Pallas kernels, shards(): pl.pallas_call(kernel, out_shape=jax.ShapeDtypeStruct(bras.shape, BF16),...  46.2 us
    unnamed x1, local copies, waits for them, and re-layouts  1.49 us

profile of v3, /device:TPU:1, one launch (start us, length us, event | category | flops | bytes accessed | tf_op | source)
XLA Modules:
  0.0 47.7 jit_solution(7407340188609463137)
XLA Ops:
  0.0 46.2 %shard_map.64 = bf16[8,4,4,208]{3,2,1,0:T(4,128)(2,1)} custom-call(bf16[8,4,4,208]{3,2,1,0:T(4,128)(2,1)} %bras_in.1, f32[1,8,4,160]{3,2,1,0:T(4,128)} %fields_in.1, bf16[1,5,21632]{2,1,0:T(8,128)(2,1)} %chol_in.1, bf16[4,21632]{1,0:T(4,128)(2,1)} %one_body_in.1, s32[2,16]{1,0:T(2,128)} %bitcast.1, s32[4,4]{1,0:T(4,128)} %kpq_in.1), custom_call_target="tpu_custom_call" | custom-call | flops 100000000 | bytes 1000000 | tf_op jit(solution)/shard_map/pallas_call | solution.py:300
  46.2 1.5 %copy.8 = bf16[8,4,4,208]{3,2,1,0:T(4,128)(2,1)} copy(bf16[8,4,4,208]{3,2,1,0:T(4,128)(2,1)} %shard_map.64) | data formatting | bytes 106496

commit v4 on v3

--- a/solution.py
+++ b/solution.py
@@ -27,7 +27,7 @@
 
 def tile_of(site, pb):
     spot = lax.rem(lax.rem(site, 2) * 8 + site // 2 + 2 * (pb // 4) + lax.rem(pb, 4), 16)
-    return spot - (spot + 1) // 3, lax.rem(spot, 3) != 1, lax.rem(site // 2 + pb, 2)
+    return spot - (spot + 1) // 3, lax.rem(spot, 3) != 1, pb // 8
 
 
 def lanes_of(shape):
@@ -108,7 +108,7 @@
     bras_in, fields_in, chol_in, one_body_in, pairs_in, kpq_in, out,
     bras, fields, chol, one_body, pairs, kpq,
     mats, obm, propagator, packed, crecv, cmat, plain, hs, hr, right, current, obuf,
-    load, hrec, csend, crec, hsend, hloc, osend, orec, ready,
+    load, hrec, csend, crec, hsend, osend, orec, ready,
 ):
     walk, pb, site, core = place()
     tile, makes, maker_core = tile_of(site, pb)
@@ -200,19 +200,11 @@
             for there in sites:
                 for to in (2 * there, 2 * there + 1):
 
-                    @pl.when((to != walk) | jnp.logical_not(active))
-                    def _():
-                        send(to, mine).start()
-
-                    def rest(di, carry):
+                    def one(di, carry):
                         send(to, lax.rem(mine + di, 8)).start()
                         return carry
 
-                    lax.fori_loop(1, 8, rest, 0)
-
-        @pl.when(active)
-        def _():
-            pltpu.make_async_copy(hs.at[walk * 8 + mine], hr.at[pb * TILES + tile], hloc).start()
+                    lax.fori_loop(0, 8, one, 0)
 
     @pl.when(active)
     def _():
@@ -222,28 +214,15 @@
         for k in range(4):
             current[k] = as_rows(summed[k])
 
-        def arrived(group, ones):
-            some = hr.at[pl.ds(group * 4 * TILES, ones)]
+        def arrived(group):
+            some = hr.at[pl.ds(group * 4 * TILES, 4 * TILES)]
             return remote(some, some, hsend, hrec.at[group], sibling, pb)
-
-        @pl.when(maker)
-        def _():
-            pltpu.make_async_copy(hs.at[walk * 8 + mine], hr.at[pb * TILES + tile], hloc).wait()
 
         for n in range(1, ORDER + 1):
             acc = [jnp.zeros((8, 256), F32) for _ in range(4)]
             for j in range(16):
                 if n == 1 and j % 4 == 0:
-                    own = maker & (pb // 4 == j // 4)
-
-                    @pl.when(own)
-                    def _():
-                        arrived(j // 4, 4 * TILES - 1).wait_recv()
-
-                    @pl.when(jnp.logical_not(own))
-                    def _():
-                        arrived(j // 4, 4 * TILES).wait_recv()
-
+                    arrived(j // 4).wait_recv()
                 if n == 1:
                     unpack(hr, right, j)
                 matrix = jnp.concatenate([hr[j * TILES : j * TILES + 8].reshape(128, 128), right[j]], axis=1)
@@ -269,30 +248,24 @@
     def _():
         remote(obuf, obuf, osend, orec, sibling, pb).wait_recv()
 
-    @pl.when(maker)
-    def _():
-        remote(packed.at[0:10], packed.at[0:10], csend, crec, sibling, pb).wait_send()
-
-        @pl.when(active)
-        def _():
-            remote(hs.at[0:255], hs.at[0:255], hsend, hrec.at[0], sibling, pb).wait_send()
-
-        @pl.when(jnp.logical_not(active))
-        def _():
-            remote(hs, hs, hsend, hrec.at[0], sibling, pb).wait_send()
-
-    @pl.when(jnp.logical_not(maker))
-    def _():
-        remote(packed, packed, csend, crec, sibling, pb).wait_send()
-
-    @pl.when(active)
-    def _():
-        remote(hs.at[0:30], hs.at[0:30], osend, orec, sibling, pb).wait_send()
-
     for w in range(8):
         rows = obuf[w].astype(F32)
         for k in range(4):
             out[w, k] = rows[4 * k : 4 * k + 4, 0 : 2 * NORB].astype(BF16)
+
+    @pl.when(maker)
+    def _():
+        remote(packed.at[0:10], packed.at[0:10], csend, crec, sibling, pb).wait_send()
+
+        remote(hs, hs, hsend, hrec.at[0], sibling, pb).wait_send()
+
+    @pl.when(jnp.logical_not(maker))
+    def _():
+        remote(packed, packed, csend, crec, sibling, pb).wait_send()
+
+    @pl.when(active)
+    def _():
+        remote(hs.at[0:30], hs.at[0:30], osend, orec, sibling, pb).wait_send()
 
 
 def shards(bras, fields, chol, one_body, pair_table, kpq_map):
@@ -323,7 +296,7 @@
             pltpu.VMEM((8, 16, 256), BF16),
             pltpu.SemaphoreType.DMA((6,)),
             pltpu.SemaphoreType.DMA((4,)),
-            *[dma] * 6,
+            *[dma] * 5,
             pltpu.SemaphoreType.REGULAR,
         ],
         compiler_params=pltpu.CompilerParams(

time: 47.9 us -> 47.6 us (level)
  no operation moved by 1% of the time
where the time goes in v4:
time: 47.6 us; the launch traced here: 47.4 us
  Pallas kernels  45.9 us (96%)
  local copies, waits for them, and re-layouts  1.49 us (3%)
    pallas_call x1, Pallas kernels, shards(): pl.pallas_call(kernel, out_shape=jax.ShapeDtypeStruct(bras.shape, BF16),...  45.9 us
    unnamed x1, local copies, waits for them, and re-layouts  1.49 us

profile of v4, /device:TPU:1, one launch (start us, length us, event | category | flops | bytes accessed | tf_op | source)
XLA Modules:
  0.0 47.4 jit_solution(12388634463574557974)
XLA Ops:
  0.0 45.9 %shard_map.64 = bf16[8,4,4,208]{3,2,1,0:T(4,128)(2,1)} custom-call(bf16[8,4,4,208]{3,2,1,0:T(4,128)(2,1)} %bras_in.1, f32[1,8,4,160]{3,2,1,0:T(4,128)} %fields_in.1, bf16[1,5,21632]{2,1,0:T(8,128)(2,1)} %chol_in.1, bf16[4,21632]{1,0:T(4,128)(2,1)} %one_body_in.1, s32[2,16]{1,0:T(2,128)} %bitcast.1, s32[4,4]{1,0:T(4,128)} %kpq_in.1), custom_call_target="tpu_custom_call" | custom-call | flops 100000000 | bytes 1000000 | tf_op jit(solution)/shard_map/pallas_call | solution.py:273
  45.9 1.5 %copy.8 = bf16[8,4,4,208]{3,2,1,0:T(4,128)(2,1)} copy(bf16[8,4,4,208]{3,2,1,0:T(4,128)(2,1)} %shard_map.64) | data formatting | bytes 106496

commit v5 on v4

--- a/solution.py
+++ b/solution.py
@@ -272,7 +272,7 @@
     dma = pltpu.SemaphoreType.DMA(())
     return pl.pallas_call(
         kernel,
-        out_shape=jax.ShapeDtypeStruct(bras.shape, BF16),
+        out_shape=pltpu.VMEM(bras.shape, BF16),
         in_specs=[pl.BlockSpec(memory_space=pltpu.HBM)] * 6,
         out_specs=pl.BlockSpec(memory_space=pltpu.VMEM),
         scratch_shapes=[

time: 47.6 us -> 46 us (0.966)
  local copies, waits for them, and re-layouts: 1.49 us -> 0.63 us
  Pallas kernels: 45.9 us -> 45.3 us
    unnamed x1, local copies, waits for them, and re-layouts: 1.49 us -> 0.63 us
    pallas_call x1, Pallas kernels: 45.9 us -> 45.3 us  [shards(): pl.pallas_call(kernel, out_shape=pltpu.VMEM(bras.shape, BF16), in_specs=[...]
where the time goes in v5:
time: 46 us; the launch traced here: 45.9 us
  Pallas kernels  45.3 us (98%)
  local copies, waits for them, and re-layouts  0.63 us (1%)
    pallas_call x1, Pallas kernels, shards(): pl.pallas_call(kernel, out_shape=pltpu.VMEM(bras.shape, BF16), in_specs=[...  45.3 us

profile of v5, /device:TPU:1, one launch (start us, length us, event | category | flops | bytes accessed | tf_op | source)
XLA Modules:
  0.0 45.9 jit_solution(1317565033031784782)
XLA Ops:
  0.0 45.3 %shard_map.64 = bf16[8,4,4,208]{3,2,1,0:T(4,128)(2,1)S(1)} custom-call(bf16[8,4,4,208]{3,2,1,0:T(4,128)(2,1)} %bras_in.1, f32[1,8,4,160]{3,2,1,0:T(4,128)} %fields_in.1, bf16[1,5,21632]{2,1,0:T(8,128)(2,1)} %chol_in.1, bf16[4,21632]{1,0:T(4,128)(2,1)} %one_body_in.1, s32[2,16]{1,0:T(2,128)} %bitcast.1, s32[4,4]{1,0:T(4,128)} %kpq_in.1), custom_call_target="tpu_custom_call" | custom-call | flops 100000000 | bytes 1000000 | tf_op jit(solution)/shard_map/pallas_call | solution.py:273
  45.3 0.6 %copy.8 = bf16[8,4,4,208]{3,2,1,0:T(4,128)(2,1)} copy(bf16[8,4,4,208]{3,2,1,0:T(4,128)(2,1)S(1)} %shard_map.64) | data formatting | bytes 106496

commit v6 on v5

--- a/solution.py
+++ b/solution.py
@@ -10,7 +10,7 @@
 TILES = 11
 PER = 5
 FAR = (12, 11, 13, 4, 10, 14, 3, 5, 9, 15, 2, 6, 8, 1, 7, 0)
-BLOCKS = ((0, 64, (0, 2, 1, 3)), (64, 256, (4, 6, 5, 8, 7, 10, 12, 14, 9, 11, 13, 15)))
+BLOCKS = ((0, 32, (0, 1)), (32, 256, (2, 3, 4, 6, 5, 8, 7, 10, 12, 14, 9, 11, 13, 15)))
 MESH = pl.DeviceIdType.MESH
 F32, BF16 = jnp.float32, jnp.bfloat16
 
@@ -162,7 +162,7 @@
 
         @pl.when(used)
         def _():
-            remote(packed.at[t], crecv.at[walk], csend, crec, there * 2 + c, pb).start()
+            remote(packed.at[t], crecv.at[walk], csend, crec.at[walk // 16], there * 2 + c, pb).start()
 
     @pl.when(maker)
     def _():
@@ -180,10 +180,20 @@
 
     @pl.when(maker)
     def _():
-        remote(crecv.at[0:31], crecv.at[0:31], csend, crec, sibling, pb).wait_recv()
-        for kg in range(10):
-            block = jnp.stack([crecv[(16 * kg + i) // PER, (16 * kg + i) % PER].astype(F32) for i in range(16)], axis=0)
-            cmat[:, 16 * kg : 16 * kg + 16, :] = jnp.transpose(block, (1, 0, 2)).astype(BF16)
+        for half in range(2):
+
+            @pl.when(walk // 16 == half)
+            def _():
+                remote(crecv.at[0:15], crecv.at[0:15], csend, crec.at[half], sibling, pb).wait_recv()
+
+            @pl.when(walk // 16 != half)
+            def _():
+                remote(crecv.at[0:16], crecv.at[0:16], csend, crec.at[half], sibling, pb).wait_recv()
+
+            for kg in range(5 * half, 5 * half + 5):
+                rows = [(16 * kg + i) // PER for i in range(16)]
+                block = jnp.stack([crecv[r, (16 * kg + i) % PER].astype(F32) for i, r in enumerate(rows)], axis=0)
+                cmat[:, 16 * kg : 16 * kg + 16, :] = jnp.transpose(block, (1, 0, 2)).astype(BF16)
         ft = crecv[:, PER].astype(F32)
         f = jnp.concatenate([ft[:, 0:8].reshape(256, 128), ft[:, 8:16].reshape(256, 128)[:, 0:32]], axis=1).astype(BF16)
         def send(to, i):
@@ -255,13 +265,13 @@
 
     @pl.when(maker)
     def _():
-        remote(packed.at[0:10], packed.at[0:10], csend, crec, sibling, pb).wait_send()
+        remote(packed.at[0:10], packed.at[0:10], csend, crec.at[0], sibling, pb).wait_send()
 
         remote(hs, hs, hsend, hrec.at[0], sibling, pb).wait_send()
 
     @pl.when(jnp.logical_not(maker))
     def _():
-        remote(packed, packed, csend, crec, sibling, pb).wait_send()
+        remote(packed, packed, csend, crec.at[0], sibling, pb).wait_send()
 
     @pl.when(active)
     def _():
@@ -296,7 +306,9 @@
             pltpu.VMEM((8, 16, 256), BF16),
             pltpu.SemaphoreType.DMA((6,)),
             pltpu.SemaphoreType.DMA((4,)),
-            *[dma] * 5,
+            dma,
+            pltpu.SemaphoreType.DMA((2,)),
+            *[dma] * 3,
             pltpu.SemaphoreType.REGULAR,
         ],
         compiler_params=pltpu.CompilerParams(

time: 46 us -> 46.1 us (level); the launches traced: 45.9 us -> 45.5 us
  no operation moved by 1% of the time
where the time goes in v6:
time: 46.1 us; the launch traced here: 45.5 us
  Pallas kernels  44.9 us (97%)
  local copies, waits for them, and re-layouts  0.63 us (1%)
    pallas_call x1, Pallas kernels, shards(): pl.pallas_call(kernel, out_shape=pltpu.VMEM(bras.shape, BF16), in_specs=[...  44.9 us

profile of v6, /device:TPU:1, one launch (start us, length us, event | category | flops | bytes accessed | tf_op | source)
XLA Modules:
  0.0 45.5 jit_solution(17141791867592975805)
XLA Ops:
  0.0 44.9 %shard_map.64 = bf16[8,4,4,208]{3,2,1,0:T(4,128)(2,1)S(1)} custom-call(bf16[8,4,4,208]{3,2,1,0:T(4,128)(2,1)} %bras_in.1, f32[1,8,4,160]{3,2,1,0:T(4,128)} %fields_in.1, bf16[1,5,21632]{2,1,0:T(8,128)(2,1)} %chol_in.1, bf16[4,21632]{1,0:T(4,128)(2,1)} %one_body_in.1, s32[2,16]{1,0:T(2,128)} %bitcast.1, s32[4,4]{1,0:T(4,128)} %kpq_in.1), custom_call_target="tpu_custom_call" | custom-call | flops 100000000 | bytes 1000000 | tf_op jit(solution)/shard_map/pallas_call | solution.py:283
  44.9 0.6 %copy.8 = bf16[8,4,4,208]{3,2,1,0:T(4,128)(2,1)} copy(bf16[8,4,4,208]{3,2,1,0:T(4,128)(2,1)S(1)} %shard_map.64) | data formatting | bytes 106496

commit v7 on v6

--- a/solution.py
+++ b/solution.py
@@ -199,6 +199,7 @@
         def send(to, i):
             return remote(hs.at[to * 8 + i], hr.at[pb * TILES + tile], hsend, hrec.at[pb // 4], to, 8 - lax.rem(to, 2) * 8 + i)
 
+        turns = [lax.rem(mine + di, 8) for di in range(8)]
         for start, stop, sites in BLOCKS:
             for p in range(0, 16, 2):
                 rhs = jnp.concatenate([cmat[p], cmat[p + 1]], axis=1)
@@ -209,6 +210,11 @@
                 hs[8 * to : 8 * to + 8] = jnp.transpose(plain[:, 8 * to : 8 * to + 8, :], (1, 0, 2)).astype(BF16)
             for there in sites:
                 for to in (2 * there, 2 * there + 1):
+
+                    if start == 0:
+                        for i in turns:
+                            send(to, i).start()
+                        continue
 
                     def one(di, carry):
                         send(to, lax.rem(mine + di, 8)).start()

time: 46.1 us -> 45.9 us (level)
  no operation moved by 1% of the time
where the time goes in v7:
time: 45.9 us; the launch traced here: 45.5 us
  Pallas kernels  44.8 us (98%)
  local copies, waits for them, and re-layouts  0.63 us (1%)
    pallas_call x1, Pallas kernels, shards(): pl.pallas_call(kernel, out_shape=pltpu.VMEM(bras.shape, BF16), in_specs=[...  44.8 us

profile of v7, /device:TPU:1, one launch (start us, length us, event | category | flops | bytes accessed | tf_op | source)
XLA Modules:
  0.0 45.5 jit_solution(13434533144200791753)
XLA Ops:
  0.0 44.8 %shard_map.64 = bf16[8,4,4,208]{3,2,1,0:T(4,128)(2,1)S(1)} custom-call(bf16[8,4,4,208]{3,2,1,0:T(4,128)(2,1)} %bras_in.1, f32[1,8,4,160]{3,2,1,0:T(4,128)} %fields_in.1, bf16[1,5,21632]{2,1,0:T(8,128)(2,1)} %chol_in.1, bf16[4,21632]{1,0:T(4,128)(2,1)} %one_body_in.1, s32[2,16]{1,0:T(2,128)} %bitcast.1, s32[4,4]{1,0:T(4,128)} %kpq_in.1), custom_call_target="tpu_custom_call" | custom-call | flops 100000000 | bytes 1000000 | tf_op jit(solution)/shard_map/pallas_call | solution.py:289
  44.8 0.6 %copy.8 = bf16[8,4,4,208]{3,2,1,0:T(4,128)(2,1)} copy(bf16[8,4,4,208]{3,2,1,0:T(4,128)(2,1)S(1)} %shard_map.64) | data formatting | bytes 106496
